TPU v7x, 32 devices: a whole 2x2x4 slice. The times are simulated.
32 devices in a mesh: gx: 4 (over y, core), ta: 8 (over z, x).
Axes of the slice: x: 2, y: 2, z: 4, core: 2. Of those that a mesh axis runs over, the one named last changes fastest.
Arguments:
- fine_field: bfloat16 [4, 8, 2048, 384], P('gx', 'ta'), may hold values from -40 to 40
- site_map: int32 [4, 8, 2048], P('gx', 'ta'), may hold values from 0 to 2047, each once within a row
- prolongator: bfloat16 [4, 8, 8, 64, 6144], P('gx', 'ta'), may hold values from -0.119628906 to 0.119628906
- coarse_op: bfloat16 [4, 8, 8, 9, 64, 64], P('gx', 'ta'), may hold values from -0.2 to 1.2
Outputs:
- correction: bfloat16 [4, 8, 2048, 384], P('gx', 'ta')
- coarse_residual: float32 [4, 8, 8, 64, 16], P('gx', 'ta')
- residual_norm: float32 [16], replicated
Inputs may be any that keep to these rules, and one draw needn't show every extreme that they name: `site_map`: each slab's row of the map names every storage row once.
All inputs are finite; a program needn't handle non-finite values.
Results may differ from a plain program's by a relative error of at most 0.013.
Values may be sent and summed in bfloat16 or wider, within the bound.
A program may use at most 64 MiB of HBM per device.

v0:
```python
import math

import jax
import jax.numpy as jnp
from jax import lax
from jax.sharding import PartitionSpec as P

SPIN = 24
XC = 4
YC = 2


def padded(block, sides, width):
    for axis, dim in sides:
        count = lax.axis_size(axis)
        forward = [(i, i + 1) for i in range(count - 1)]
        forward.append((count - 1, 0))
        backward = [(target, source) for source, target in forward]
        low = lax.ppermute(
            lax.slice_in_dim(block, block.shape[dim] - width, None, axis=dim), axis, forward
        )
        high = lax.ppermute(lax.slice_in_dim(block, 0, width, axis=dim), axis, backward)
        block = jnp.concatenate([low, block, high], axis=dim)
    return block


def plane_hops(vector):
    grid = vector.reshape(
        vector.shape[0], vector.shape[1], XC, YC, vector.shape[3], vector.shape[4]
    )

    def flatten(values):
        return values.reshape(vector.shape)

    return [
        vector,
        flatten(jnp.roll(grid, -1, 2)),
        flatten(jnp.roll(grid, 1, 2)),
        flatten(jnp.roll(grid, -1, 3)),
        flatten(jnp.roll(grid, 1, 3)),
    ]


def apply_blocks(coarse_op, neighbours):
    result = jnp.einsum(
        "ztaij,ztajr->ztair",
        coarse_op[:, :, :, 0],
        neighbours[0],
        preferred_element_type=jnp.float32,
    )
    for hop_index in range(1, 9):
        result = result + jnp.einsum(
            "ztaij,ztajr->ztair",
            coarse_op[:, :, :, hop_index],
            neighbours[hop_index],
            preferred_element_type=jnp.float32,
        )
    return result


def spread_hops(vector):
    padded_z = padded(vector, (("gx", 0),), 1)
    padded_t = padded(vector, (("ta", 1),), 1)
    along_z = [padded_z[2:], padded_z[:-2]]
    along_t = [padded_t[:, 2:], padded_t[:, :-2]]
    return plane_hops(vector) + along_z + along_t


def richardson_pair(coarse_op, restricted, hop_maker):
    start_values = restricted.astype(jnp.float32)
    first_iter = (0.5 * start_values).astype(jnp.bfloat16)
    first_resid = start_values - apply_blocks(coarse_op, hop_maker(first_iter))
    second_iter = (first_iter.astype(jnp.float32) + 0.5 * first_resid).astype(jnp.bfloat16)
    residual_two = start_values - apply_blocks(coarse_op, hop_maker(second_iter))
    third_iter = (second_iter.astype(jnp.float32) + 0.5 * residual_two).astype(jnp.bfloat16)
    return (residual_two, third_iter)


def permute_rows(values, site_map, inverse):
    rows = values.shape[2]
    block = math.gcd(512, rows)
    count = rows // block
    positions = jnp.arange(rows, dtype=jnp.int32)

    def one_block(index):
        start = index * block
        if inverse:
            targets = lax.dynamic_slice_in_dim(positions, start, block, 0)
            table = targets[None, None, :, None] == site_map[:, :, None, :]
        else:
            picks = lax.dynamic_slice_in_dim(site_map, start, block, 2)
            table = picks[:, :, :, None] == positions[None, None, None, :]
        return jnp.einsum(
            "ztbk,ztkc->ztbc",
            table.astype(jnp.bfloat16),
            values,
            preferred_element_type=jnp.float32,
        ).astype(jnp.bfloat16)

    blocks = lax.map(one_block, jnp.arange(count, dtype=jnp.int32))
    return jnp.moveaxis(blocks, 0, 2).reshape(values.shape)


def local(fine_field, site_map, prolongator, coarse_op):
    slabs_z, slabs_t = (fine_field.shape[0], fine_field.shape[1])
    aggregates = prolongator.shape[2]
    columns = fine_field.shape[3]
    rhs_count = columns // SPIN
    ordered = permute_rows(fine_field, site_map, False)
    ordered = ordered.reshape(slabs_z, slabs_t, aggregates, prolongator.shape[4], rhs_count)
    restricted = jnp.einsum(
        "ztacm,ztamr->ztacr", prolongator, ordered, preferred_element_type=jnp.float32
    ).astype(jnp.bfloat16)
    coarse_residual, third_iter = richardson_pair(coarse_op, restricted, spread_hops)
    squares = lax.psum(jnp.sum(coarse_residual * coarse_residual, axis=(0, 1, 2, 3)), ("gx", "ta"))
    residual_norm = jnp.sqrt(squares + 1e-06)
    lifted = jnp.einsum(
        "ztacm,ztacr->ztamr", prolongator, third_iter, preferred_element_type=jnp.float32
    ).astype(jnp.bfloat16)
    lifted = lifted.reshape(slabs_z, slabs_t, fine_field.shape[2], columns)
    correction = permute_rows(lifted, site_map, True)
    return (correction, coarse_residual, residual_norm)


def solution(mesh):
    placed = (
        P("gx", "ta", None, None),
        P("gx", "ta", None),
        P("gx", "ta", None, None, None),
        P("gx", "ta", None, None, None, None),
    )
    return jax.shard_map(
        local,
        mesh=mesh,
        in_specs=placed,
        out_specs=(P("gx", "ta", None, None), P("gx", "ta", None, None, None), P()),
        check_vma=False,
    )
```

profile of v0, /device:TPU:0, one launch (start us, length us, event | category | flops | bytes accessed | tf_op | source)
XLA Modules:
  0.0 131.3 jit_solution(6606469171203009899)
XLA Ops:
  0.8 0.5 copy-done.3
  1.3 16.1 %while.22 = (s32[]{:T(128)}, bf16[4,1,1,512,384]{4,3,2,1,0:T(8,128)(2,1)S(1)}, s32[4]{0:T(128)S(1)}, s32[1,1,2048]{2,1,0:T(1,128)S(1)}, bf16[1,1,2048,384]{3,2,1...) while((s32[]{:T(128)}, bf16[4,1,1,512,384]{4,3,2,1,0:T(8,128)(2,1)S(1)}, ...), condition=%wide.region_1.2_spmd.clone, body=%wide.region_0.1_spmd.clone.sunk | while | flops 806551552 | bytes 1972383 | solution.py:100
  1.3 0.6 dynamic_slice.26
  2.6 2.8 %fusion.151 = bf16[4,1,1,512,384]{4,3,2,1,0:T(8,128)(2,1)S(1)} fusion(bf16[4,1,1,512,384]{4,3,2,1,0:T(8,128)(2,1)S(1)} %get-tuple-element.199, s32[]{:T(128)} %get-tuple-element.198, bf16[1,1,2048,384]{3,2,1,0:T(8,128)(2,1)} %get-tuple-element.211, s32[512]{0:T(512)S(1)} %bitcast.242), kind=kOutput, calls=%fused_computation.17.clone.1 | convolution fusion | flops 806551552 | bytes 1968132 | tf_op jit(solution)/shard_map/while/body/eval_jaxpr/ztbk,ztkc->ztbc/dot_general | solution.py:93
  5.4 0.6 dynamic_slice.26
  6.6 2.8 %fusion.151 = bf16[4,1,1,512,384]{4,3,2,1,0:T(8,128)(2,1)S(1)} fusion(bf16[4,1,1,512,384]{4,3,2,1,0:T(8,128)(2,1)S(1)} %get-tuple-element.199, s32[]{:T(128)} %get-tuple-element.198, bf16[1,1,2048,384]{3,2,1,0:T(8,128)(2,1)} %get-tuple-element.211, s32[512]{0:T(512)S(1)} %bitcast.242), kind=kOutput, calls=%fused_computation.17.clone.1 | convolution fusion | flops 806551552 | bytes 1968132 | tf_op jit(solution)/shard_map/while/body/eval_jaxpr/ztbk,ztkc->ztbc/dot_general | solution.py:93
  9.4 0.6 dynamic_slice.26
  10.7 2.8 %fusion.151 = bf16[4,1,1,512,384]{4,3,2,1,0:T(8,128)(2,1)S(1)} fusion(bf16[4,1,1,512,384]{4,3,2,1,0:T(8,128)(2,1)S(1)} %get-tuple-element.199, s32[]{:T(128)} %get-tuple-element.198, bf16[1,1,2048,384]{3,2,1,0:T(8,128)(2,1)} %get-tuple-element.211, s32[512]{0:T(512)S(1)} %bitcast.242), kind=kOutput, calls=%fused_computation.17.clone.1 | convolution fusion | flops 806551552 | bytes 1968132 | tf_op jit(solution)/shard_map/while/body/eval_jaxpr/ztbk,ztkc->ztbc/dot_general | solution.py:93
  13.4 0.6 dynamic_slice.26
  14.7 2.8 %fusion.151 = bf16[4,1,1,512,384]{4,3,2,1,0:T(8,128)(2,1)S(1)} fusion(bf16[4,1,1,512,384]{4,3,2,1,0:T(8,128)(2,1)S(1)} %get-tuple-element.199, s32[]{:T(128)} %get-tuple-element.198, bf16[1,1,2048,384]{3,2,1,0:T(8,128)(2,1)} %get-tuple-element.211, s32[512]{0:T(512)S(1)} %bitcast.242), kind=kOutput, calls=%fused_computation.17.clone.1 | convolution fusion | flops 806551552 | bytes 1968132 | tf_op jit(solution)/shard_map/while/body/eval_jaxpr/ztbk,ztkc->ztbc/dot_general | solution.py:93
  17.5 10.9 %reshape.364 = bf16[8,6144,16]{2,1,0:T(8,128)(2,1)} reshape(bf16[4,1,1,512,384]{4,3,2,1,0:T(8,128)(2,1)S(1)} %get-tuple-element.67) | data formatting | bytes 3145728 | tf_op jit(solution)/shard_map/reshape.22
  28.4 8.3 %multiply_convert_fusion = (bf16[8,16,64]{2,1,0:T(8,128)(2,1)S(1)}, f32[8,16,64]{2,1,0:T(8,128)S(1)}) fusion(bf16[8,6144,16]{2,1,0:T(8,128)(2,1)} %reshape.364, bf16[1,1,8,64,6144]{4,3,2,1,0:T(8,128)(2,1)} %param.10), kind=kOutput, calls=%fused_computation.97 | convolution fusion | flops 100696064 | bytes 7913472 | tf_op jit(solution)/shard_map/ztacm,ztamr->ztacr/dot_general | solution.py:111
  36.6 3.0 %collective-permute-start.3 = (bf16[1,1,8,64,16]{3,4,2,1,0:T(8,128)(2,1)S(1)}, bf16[1,1,8,64,16]{3,4,2,1,0:T(8,128)(2,1)S(1)}, u32[]{:S(2)}, u32[]{:S(2)}) collective-permute-start(bf16[1,1,8,64,16]{3,4,2,1,0:T(8,128)(2,1)S(1)} %bitcast.226), channel_id=1, source_target_pairs={{0,1},{1,2},{2,3},{3,4},{4,5},{5,6},{6,7},{7,0},{8,9},{9,10},{10,1... | collective-permute-start | bytes 49160 | tf_op jit(solution)/shard_map/ppermute | solution.py:19
  39.6 3.1 %collective-permute-start.2 = (bf16[1,1,8,64,16]{3,4,2,1,0:T(8,128)(2,1)S(1)}, bf16[1,1,8,64,16]{3,4,2,1,0:T(8,128)(2,1)S(1)}, u32[]{:S(2)}, u32[]{:S(2)}) collective-permute-start(bf16[1,1,8,64,16]{3,4,2,1,0:T(8,128)(2,1)S(1)} %bitcast.227), channel_id=1, source_target_pairs={{1,0},{2,1},{3,2},{4,3},{5,4},{6,5},{7,6},{0,7},{9,8},{10,9},{11,1... | collective-permute-start | bytes 49160 | tf_op jit(solution)/shard_map/ppermute | solution.py:22
  42.7 1.7 %collective-permute-start = (bf16[1,1,8,64,16]{3,4,2,1,0:T(8,128)(2,1)S(1)}, bf16[1,1,8,64,16]{3,4,2,1,0:T(8,128)(2,1)S(1)}, u32[]{:S(2)}, u32[]{:S(2)}) collective-permute-start(bf16[1,1,8,64,16]{3,4,2,1,0:T(8,128)(2,1)S(1)} %bitcast.229), channel_id=1, source_target_pairs={{8,0},{16,8},{24,16},{0,24},{9,1},{17,9},{25,17},{1,25},{10,2},{18... | collective-permute-start | bytes 49160 | tf_op jit(solution)/shard_map/ppermute | solution.py:22
  46.7 4.6 %collective-permute-start.6 = (bf16[1,1,8,64,16]{3,4,2,1,0:T(8,128)(2,1)S(1)}, bf16[1,1,8,64,16]{3,4,2,1,0:T(8,128)(2,1)S(1)}, u32[]{:S(2)}, u32[]{:S(2)}) collective-permute-start(bf16[1,1,8,64,16]{3,4,2,1,0:T(8,128)(2,1)S(1)} %bitcast.223), channel_id=1, source_target_pairs={{1,0},{2,1},{3,2},{4,3},{5,4},{6,5},{7,6},{0,7},{9,8},{10,9},{11,1... | collective-permute-start | bytes 49160 | tf_op jit(solution)/shard_map/ppermute | solution.py:22
  51.3 1.0 collective-permute-start.5
  52.4 0.7 collective-permute-start.4
  55.2 3.7 %fusion.43 = bf16[8,6144,16]{1,2,0:T(8,128)(2,1)S(1)} fusion(bf16[1,1,8,64,6144]{4,3,2,1,0:T(8,128)(2,1)} %param.10, f32[8,16,64]{2,1,0:T(8,128)S(1)} %get-tuple-element.118, bf16[8,64,16]{1,2,0:T(8,128)(2,1)S(1)} %fusion.64), kind=kOutput, calls=%fused_computation.20 | convolution fusion | flops 101482496 | bytes 7913472 | tf_op jit(solution)/shard_map/ztacm,ztacr->ztamr/dot_general | solution.py:117
  58.9 8.1 %copy.27 = bf16[8,6144,16]{2,1,0:T(8,128)(2,1)} copy(bf16[8,6144,16]{1,2,0:T(8,128)(2,1)S(1)} %fusion.43) | data formatting | bytes 3145728 | tf_op jit(solution)/shard_map/convert_element_type | solution.py:119
  67.1 13.7 %reshape.391 = bf16[1,1,2048,384]{3,2,1,0:T(8,128)(2,1)S(1)} reshape(bf16[8,6144,16]{2,1,0:T(8,128)(2,1)} %copy.27) | data formatting | bytes 3145728 | tf_op jit(solution)/shard_map/reshape | solution.py:120
  81.0 10.8 %while.21 = (s32[]{:T(128)}, bf16[4,1,1,512,384]{4,3,2,1,0:T(8,128)(2,1)S(1)}, s32[4]{0:T(128)S(1)}, s32[2048]{0:T(1024)S(1)}, s32[1,1,2048]{2,1,0:T(1,128)S(1)}...) while((s32[]{:T(128)}, ...), condition=%wide.region_3.4_spmd, body=%wide.region_2.3_spmd.sunk | while | flops 806551552 | bytes 1980583 | solution.py:100
  81.0 0.6 dynamic_slice.23
  82.3 1.3 %fusion.148 = bf16[4,1,1,512,384]{4,3,2,1,0:T(8,128)(2,1)S(1)} fusion(bf16[4,1,1,512,384]{4,3,2,1,0:T(8,128)(2,1)S(1)} %get-tuple-element.227, s32[]{:T(128)} %get-tuple-element.226, bf16[1,1,2048,384]{3,2,1,0:T(8,128)(2,1)S(1)} %get-tuple-element.241, s32[2048]{0:T(1024)S(1)} %bitcast.243, s32[512]{0:T(512)S(1)} %dynamic_slice.24), kind=kOutput, calls=%fused_computation.9.clone.1 | convolution fusion | flops 806551552 | bytes 1976324 | tf_op jit(solution)/shard_map/while/body/eval_jaxpr/ztbk,ztkc->ztbc/dot_general | solution.py:93
  83.7 0.6 dynamic_slice.23
  85.0 1.3 %fusion.148 = bf16[4,1,1,512,384]{4,3,2,1,0:T(8,128)(2,1)S(1)} fusion(bf16[4,1,1,512,384]{4,3,2,1,0:T(8,128)(2,1)S(1)} %get-tuple-element.227, s32[]{:T(128)} %get-tuple-element.226, bf16[1,1,2048,384]{3,2,1,0:T(8,128)(2,1)S(1)} %get-tuple-element.241, s32[2048]{0:T(1024)S(1)} %bitcast.243, s32[512]{0:T(512)S(1)} %dynamic_slice.24), kind=kOutput, calls=%fused_computation.9.clone.1 | convolution fusion | flops 806551552 | bytes 1976324 | tf_op jit(solution)/shard_map/while/body/eval_jaxpr/ztbk,ztkc->ztbc/dot_general | solution.py:93
  86.4 0.6 dynamic_slice.23
  87.7 1.3 %fusion.148 = bf16[4,1,1,512,384]{4,3,2,1,0:T(8,128)(2,1)S(1)} fusion(bf16[4,1,1,512,384]{4,3,2,1,0:T(8,128)(2,1)S(1)} %get-tuple-element.227, s32[]{:T(128)} %get-tuple-element.226, bf16[1,1,2048,384]{3,2,1,0:T(8,128)(2,1)S(1)} %get-tuple-element.241, s32[2048]{0:T(1024)S(1)} %bitcast.243, s32[512]{0:T(512)S(1)} %dynamic_slice.24), kind=kOutput, calls=%fused_computation.9.clone.1 | convolution fusion | flops 806551552 | bytes 1976324 | tf_op jit(solution)/shard_map/while/body/eval_jaxpr/ztbk,ztkc->ztbc/dot_general | solution.py:93
  89.1 0.6 dynamic_slice.23
  90.4 1.3 %fusion.148 = bf16[4,1,1,512,384]{4,3,2,1,0:T(8,128)(2,1)S(1)} fusion(bf16[4,1,1,512,384]{4,3,2,1,0:T(8,128)(2,1)S(1)} %get-tuple-element.227, s32[]{:T(128)} %get-tuple-element.226, bf16[1,1,2048,384]{3,2,1,0:T(8,128)(2,1)S(1)} %get-tuple-element.241, s32[2048]{0:T(1024)S(1)} %bitcast.243, s32[512]{0:T(512)S(1)} %dynamic_slice.24), kind=kOutput, calls=%fused_computation.9.clone.1 | convolution fusion | flops 806551552 | bytes 1976324 | tf_op jit(solution)/shard_map/while/body/eval_jaxpr/ztbk,ztkc->ztbc/dot_general | solution.py:93
  91.7 39.0 %psum.7 = f32[16]{0:T(128)S(1)} all-reduce(f32[16]{0:T(128)S(1)} %get-tuple-element.117), channel_id=1, replica_groups=mesh['gx'=4,'ta'=8] {'gx','ta'}, use_global_device_ids=true, to_apply=%region_5.6 | all-reduce | flops 16 | bytes 128 | tf_op jit(solution)/shard_map/psum | solution.py:115
  130.8 0.5 add_sqrt_fusion
  (59 shorter events, 5.0 us)
Async XLA Ops:
  0.6 0.7 copy-start.3
  28.4 16.1 %copy-start = (bf16[1,1,8,9,64,64]{5,4,3,2,1,0:T(8,128)(2,1)S(1)}, bf16[1,1,8,9,64,64]{5,4,3,2,1,0:T(8,128)(2,1)}, u32[]{:S(2)}) copy-start(bf16[1,1,8,9,64,64]{5,4,3,2,1,0:T(8,128)(2,1)} %param.11) | copy-start | bytes 1769476
  36.6 8.8 %collective-permute-start.3 = (bf16[1,1,8,64,16]{3,4,2,1,0:T(8,128)(2,1)S(1)}, bf16[1,1,8,64,16]{3,4,2,1,0:T(8,128)(2,1)S(1)}, u32[]{:S(2)}, u32[]{:S(2)}) collective-permute-start(bf16[1,1,8,64,16]{3,4,2,1,0:T(8,128)(2,1)S(1)} %bitcast.226), channel_id=1, source_target_pairs={{0,1},{1,2},{2,3},{3,4},{4,5},{5,6},{6,7},{7,0},{8,9},{9,10},{10,1... | collective-permute-start | bytes 49160 | tf_op jit(solution)/shard_map/ppermute | solution.py:19
  39.6 6.0 %collective-permute-start.2 = (bf16[1,1,8,64,16]{3,4,2,1,0:T(8,128)(2,1)S(1)}, bf16[1,1,8,64,16]{3,4,2,1,0:T(8,128)(2,1)S(1)}, u32[]{:S(2)}, u32[]{:S(2)}) collective-permute-start(bf16[1,1,8,64,16]{3,4,2,1,0:T(8,128)(2,1)S(1)} %bitcast.227), channel_id=1, source_target_pairs={{1,0},{2,1},{3,2},{4,3},{5,4},{6,5},{7,6},{0,7},{9,8},{10,9},{11,1... | collective-permute-start | bytes 49160 | tf_op jit(solution)/shard_map/ppermute | solution.py:22
  42.7 3.3 %collective-permute-start.1 = (bf16[1,1,8,64,16]{3,4,2,1,0:T(8,128)(2,1)S(1)}, bf16[1,1,8,64,16]{3,4,2,1,0:T(8,128)(2,1)S(1)}, u32[]{:S(2)}, u32[]{:S(2)}) collective-permute-start(bf16[1,1,8,64,16]{3,4,2,1,0:T(8,128)(2,1)S(1)} %bitcast.228), channel_id=1, source_target_pairs={{0,8},{8,16},{16,24},{24,0},{1,9},{9,17},{17,25},{25,1},{2,10},{10... | collective-permute-start | bytes 49160 | tf_op jit(solution)/shard_map/ppermute | solution.py:19
  42.7 3.5 %collective-permute-start = (bf16[1,1,8,64,16]{3,4,2,1,0:T(8,128)(2,1)S(1)}, bf16[1,1,8,64,16]{3,4,2,1,0:T(8,128)(2,1)S(1)}, u32[]{:S(2)}, u32[]{:S(2)}) collective-permute-start(bf16[1,1,8,64,16]{3,4,2,1,0:T(8,128)(2,1)S(1)} %bitcast.229), channel_id=1, source_target_pairs={{8,0},{16,8},{24,16},{0,24},{9,1},{17,9},{25,17},{1,25},{10,2},{18... | collective-permute-start | bytes 49160 | tf_op jit(solution)/shard_map/ppermute | solution.py:22
  46.6 7.3 %collective-permute-start.7 = (bf16[1,1,8,64,16]{3,4,2,1,0:T(8,128)(2,1)S(1)}, bf16[1,1,8,64,16]{3,4,2,1,0:T(8,128)(2,1)S(1)}, u32[]{:S(2)}, u32[]{:S(2)}) collective-permute-start(bf16[1,1,8,64,16]{3,4,2,1,0:T(8,128)(2,1)S(1)} %bitcast.222), channel_id=1, source_target_pairs={{0,1},{1,2},{2,3},{3,4},{4,5},{5,6},{6,7},{7,0},{8,9},{9,10},{10,1... | collective-permute-start | bytes 49160 | tf_op jit(solution)/shard_map/ppermute | solution.py:19
  46.7 7.3 %collective-permute-start.6 = (bf16[1,1,8,64,16]{3,4,2,1,0:T(8,128)(2,1)S(1)}, bf16[1,1,8,64,16]{3,4,2,1,0:T(8,128)(2,1)S(1)}, u32[]{:S(2)}, u32[]{:S(2)}) collective-permute-start(bf16[1,1,8,64,16]{3,4,2,1,0:T(8,128)(2,1)S(1)} %bitcast.223), channel_id=1, source_target_pairs={{1,0},{2,1},{3,2},{4,3},{5,4},{6,5},{7,6},{0,7},{9,8},{10,9},{11,1... | collective-permute-start | bytes 49160 | tf_op jit(solution)/shard_map/ppermute | solution.py:22
  51.3 3.3 %collective-permute-start.5 = (bf16[1,1,8,64,16]{3,4,2,1,0:T(8,128)(2,1)S(1)}, bf16[1,1,8,64,16]{3,4,2,1,0:T(8,128)(2,1)S(1)}, u32[]{:S(2)}, u32[]{:S(2)}) collective-permute-start(bf16[1,1,8,64,16]{3,4,2,1,0:T(8,128)(2,1)S(1)} %bitcast.224), channel_id=1, source_target_pairs={{0,8},{8,16},{16,24},{24,0},{1,9},{9,17},{17,25},{25,1},{2,10},{10... | collective-permute-start | bytes 49160 | tf_op jit(solution)/shard_map/ppermute | solution.py:19
  52.4 2.5 %collective-permute-start.4 = (bf16[1,1,8,64,16]{3,4,2,1,0:T(8,128)(2,1)S(1)}, bf16[1,1,8,64,16]{3,4,2,1,0:T(8,128)(2,1)S(1)}, u32[]{:S(2)}, u32[]{:S(2)}) collective-permute-start(bf16[1,1,8,64,16]{3,4,2,1,0:T(8,128)(2,1)S(1)} %bitcast.225), channel_id=1, source_target_pairs={{8,0},{16,8},{24,16},{0,24},{9,1},{17,9},{25,17},{1,25},{10,2},{18... | collective-permute-start | bytes 49160 | tf_op jit(solution)/shard_map/ppermute | solution.py:22
  55.2 3.8 %copy-start.2 = (f32[8,16,64]{2,1,0:T(8,128)}, f32[8,16,64]{2,1,0:T(8,128)S(1)}, u32[]{:S(2)}) copy-start(f32[8,16,64]{2,1,0:T(8,128)S(1)} %get-tuple-element.118) | copy-start | bytes 98308
  91.7 39.6 %copy-start.1 = (bf16[4,1,1,512,384]{4,3,2,1,0:T(8,128)(2,1)}, bf16[4,1,1,512,384]{4,3,2,1,0:T(8,128)(2,1)S(1)}, u32[]{:S(2)}) copy-start(bf16[4,1,1,512,384]{4,3,2,1,0:T(8,128)(2,1)S(1)} %get-tuple-element.68) | copy-start | bytes 4718596
where the time goes:
time: 132 us; the launch traced here: 131 us
  blocking collectives  39 us (30%)
  local copies, waits for them, and re-layouts  38.6 us (29%)
  matrix products  31.8 us (24%)
  starting transfers between devices  14.3 us (11%)
  loops' own time  5.44 us (4%)
    psum x1, blocking collectives, local(): lax.psum(jnp.sum(coarse_residual * coarse_residual, axis=(0, 1, 2, 3)), (...  39 us
    dot_general x8, matrix products, one_block(): jnp.einsum('ztbk,ztkc->ztbc', table.astype(jnp.bfloat16), values, preferr...  16.4 us
    reshape x1, local copies, waits for them, and re-layouts, local(): lifted = lifted.reshape(slabs_z, slabs_t, fine_field.shape[2], columns)  13.7 us
    another operation x3, local copies, waits for them, and re-layouts  11.2 us
    ppermute x4, starting transfers between devices, padded(): lax.ppermute(lax.slice_in_dim(block, 0, width, axis=dim), axis, backward)  10.1 us
    dot_general x1, matrix products, local(): jnp.einsum('ztacm,ztamr->ztacr', prolongator, ordered, preferred_element_...  8.26 us
    convert_element_type x1, local copies, waits for them, and re-layouts, local(): lifted = jnp.einsum('ztacm,ztacr->ztamr', prolongator, third_iter, prefer...  8.15 us
    another operation x2, loops' own time, permute_rows(): blocks = lax.map(one_block, jnp.arange(count, dtype=jnp.int32))  5.44 us
  transfers between devices with their start and end apart: 8, of which 2 were waited for; matrix products, arithmetic and copies ran while one was open for 2% of the time, Pallas kernels for 0%

commit v1 on v0

v1 whole, which is shorter than its diff:
```python
import functools

import jax
import jax.numpy as jnp
from jax import lax
from jax.experimental import pallas as pl
from jax.experimental.pallas import tpu as pltpu
from jax.sharding import PartitionSpec as P

SPIN = 24
XC = 4
YC = 2
SITES = XC * YC
LANES = 128
RHS = 16
STEP = 32
MESH = pl.DeviceIdType.MESH


def lane_group(shape):
    return lax.broadcasted_iota(jnp.int32, shape, len(shape) - 1) // RHS


def restrict_kernel(map_ref, fine_ref, prol_ref, rest_ref, wide):
    agg = pl.program_id(0)
    rows = fine_ref.shape[2]
    sites = rows // SITES

    @pl.when(agg == 0)
    def _():
        def widen(index, carry):
            at = pl.ds(pl.multiple_of(index * 64, 64), 64)
            for g in range(3):
                wide[g, at, :] = fine_ref[0, 0, at, g * LANES:(g + 1) * LANES].astype(jnp.float32)
            return carry
        lax.fori_loop(0, rows // 64, widen, 0)

    diagonal = lax.broadcasted_iota(jnp.int32, (8, LANES), 0) == lane_group((8, LANES))

    def body(chunk, acc):
        parts = []
        for k in range(STEP):
            row = map_ref[0, 0, agg * sites + chunk * STEP + k]
            for g in range(3):
                one = jnp.broadcast_to(wide[g, pl.ds(row, 1), :], (8, LANES))
                parts.append(jnp.where(diagonal, one, 0.0))
        tiles = [
            jnp.concatenate(parts[i:i + 2], axis=0).astype(jnp.bfloat16)
            for i in range(0, len(parts), 2)
        ]
        spread = jnp.concatenate(tiles, axis=0)
        width = STEP * SPIN
        block = prol_ref[0, 0, 0, :, pl.ds(pl.multiple_of(chunk * width, width), width)]
        return acc + jnp.dot(block, spread, preferred_element_type=jnp.float32)

    coarse = prol_ref.shape[3]
    acc = lax.fori_loop(0, sites // STEP, body, jnp.zeros((coarse, LANES), jnp.float32))
    for shift in (16, 32, 64):
        acc = acc + pltpu.roll(acc, shift, 1)
    acc = acc.astype(jnp.bfloat16).astype(jnp.float32)
    group = lane_group(acc.shape)
    rest_ref[...] = jnp.where(group == agg, acc, rest_ref[...])


def richardson_kernel(
    nz, nt, rest_ref, op_ref, resid_ref, norm_ref, third_ref,
    packed, sent, halo, part, sums_z, sums_t,
    send_sem, recv_sem, zs_sem, zr_sem, ts_sem, tr_sem,
):
    z, t = lax.axis_index("gx"), lax.axis_index("ta")
    barrier = pltpu.get_barrier_semaphore()
    for d in range(1, nz):
        pl.semaphore_signal(barrier, inc=1, device_id=(lax.rem(z + d, nz), t), device_id_type=MESH)
    for d in range(1, nt):
        pl.semaphore_signal(barrier, inc=1, device_id=(z, lax.rem(t + d, nt)), device_id_type=MESH)

    rest = rest_ref[...]
    coarse = rest.shape[0]
    first = 0.5 * rest
    sent[0] = first.astype(jnp.bfloat16)

    targets = (
        (lax.rem(z + nz - 1, nz), t),
        (lax.rem(z + 1, nz), t),
        (z, lax.rem(t + nt - 1, nt)),
        (z, lax.rem(t + 1, nt)),
    )

    def exchange(turn):
        copies = []
        for slot, target in enumerate(targets):
            copy = pltpu.make_async_remote_copy(
                src_ref=sent.at[turn],
                dst_ref=halo.at[turn, pl.ds(slot * coarse, coarse)],
                send_sem=send_sem.at[turn, slot],
                recv_sem=recv_sem.at[turn, slot],
                device_id=target,
                device_id_type=MESH,
            )
            copy.start()
            copies.append(copy)
        return copies

    group = lane_group(rest.shape)
    even = lax.rem(group, 2) == 0

    def pick(full):
        result = full[0:coarse]
        for s in range(1, SITES):
            result = jnp.where(group == s, full[s * coarse:(s + 1) * coarse], result)
        return result

    def apply_blocks(values, turn, copies):
        up = pltpu.roll(values, LANES - YC * RHS, 1)
        down = pltpu.roll(values, YC * RHS, 1)
        swap = jnp.where(even, pltpu.roll(values, LANES - RHS, 1), pltpu.roll(values, RHS, 1))
        zero = jnp.zeros_like(values)
        stack = jnp.concatenate([values, up, down, swap, swap, zero], axis=0).astype(jnp.bfloat16)
        full = jnp.dot(packed[:, 4 * coarse:], stack, preferred_element_type=jnp.float32)
        near = pick(full)
        for copy in copies:
            copy.wait()
        far = jnp.dot(packed[:, :4 * coarse], halo[turn], preferred_element_type=jnp.float32)
        return near + pick(far)

    pl.semaphore_wait(barrier, nz - 1 + nt - 1)
    copies = exchange(0)
    for h in range(9):
        at = (h - 5 if h >= 5 else h + 4) * coarse
        for s in range(SITES):
            packed[s * coarse:(s + 1) * coarse, at:at + coarse] = op_ref[0, 0, s, h]
    packed[:, 9 * coarse:] = jnp.zeros((SITES * coarse, coarse), jnp.bfloat16)
    first_resid = rest - apply_blocks(first, 0, copies)
    second_low = (first + 0.5 * first_resid).astype(jnp.bfloat16)
    sent[1] = second_low
    copies = exchange(1)
    second = second_low.astype(jnp.float32)
    resid = rest - apply_blocks(second, 1, copies)

    total = jnp.sum((resid * resid).reshape(coarse // 8, 8, LANES), axis=0)
    for shift in (16, 32, 64):
        total = total + pltpu.roll(total, shift, 1)
    part[0] = total

    def gather(turn, count, device, sums, s_sem, r_sem):
        pending = []
        for d in range(1, count):
            copy = pltpu.make_async_remote_copy(
                src_ref=part.at[turn],
                dst_ref=sums.at[d - 1],
                send_sem=s_sem.at[d - 1],
                recv_sem=r_sem.at[d - 1],
                device_id=device(d),
                device_id_type=MESH,
            )
            copy.start()
            pending.append(copy)
        return pending

    along_z = gather(0, nz, lambda d: (lax.rem(z + d, nz), t), sums_z, zs_sem, zr_sem)
    third = (second + 0.5 * resid).astype(jnp.bfloat16).astype(jnp.float32)
    third_ref[...] = jnp.transpose(third).astype(jnp.bfloat16)
    for copy in along_z:
        copy.wait()
    for d in range(nz - 1):
        total = total + sums_z[d]
    part[1] = total
    along_t = gather(1, nt, lambda d: (z, lax.rem(t + d, nt)), sums_t, ts_sem, tr_sem)
    for s in range(SITES):
        resid_ref[0, 0, s] = resid[:, s * RHS:(s + 1) * RHS]
    for copy in along_t:
        copy.wait()
    for d in range(nt - 1):
        total = total + sums_t[d]
    norm_ref[...] = jnp.sqrt(jnp.sum(total, axis=0, keepdims=True) + 1e-06)


def lift_kernel(map_ref, third_ref, prol_ref, out_ref, held, placed):
    agg = pl.program_id(0)
    rows = out_ref.shape[2]
    sites = rows // SITES
    values = third_ref[pl.ds(pl.multiple_of(agg * RHS, RHS), RHS), :]
    masks = [
        (lax.rem(lax.broadcasted_iota(jnp.int32, (RHS, 256), 1), 8) == i)
        .astype(jnp.float32).astype(jnp.bfloat16)
        for i in range(8)
    ]
    folds = (
        lax.broadcasted_iota(jnp.int32, (32, 256), 0)
        == lax.broadcasted_iota(jnp.int32, (32, 256), 1) // 8
    ).astype(jnp.float32).astype(jnp.bfloat16)
    width = STEP * SPIN

    def body(chunk, carry):
        block = prol_ref[0, 0, 0, :, pl.ds(pl.multiple_of(chunk * width, width), width)]
        flat = jnp.dot(values, block, preferred_element_type=jnp.float32).astype(jnp.bfloat16)
        base = chunk * (width // 8)
        for u in range(width // 256):
            piece = flat[:, u * 256:(u + 1) * 256]
            spread = jnp.concatenate([piece * masks[i] for i in range(8)], axis=0)
            held[pl.ds(pl.multiple_of(base + u * 32, 32), 32), :] = lax.dot_general(
                folds, spread, (((1,), (1,)), ((), ())), preferred_element_type=jnp.float32
            )
        for k in range(STEP):
            row = map_ref[0, 0, agg * sites + chunk * STEP + k]
            placed[pl.ds(pl.multiple_of(row * 8, 8), 8), :] = held[pl.ds(base + 3 * k, 8), :]
        return carry

    lax.fori_loop(0, sites // STEP, body, 0)

    @pl.when(agg == SITES - 1)
    def _():
        def narrow(index, carry):
            at = pl.ds(pl.multiple_of(index * 64, 64), 64)
            for g in range(3):
                out_ref[0, 0, at, g * LANES:(g + 1) * LANES] = placed[
                    pl.ds(index * 512 + g, 64, stride=8), :
                ].astype(jnp.bfloat16)
            return carry
        lax.fori_loop(0, rows // 64, narrow, 0)


def local(nz, nt, fine_field, site_map, prolongator, coarse_op):
    rows, columns = fine_field.shape[2:]
    coarse, depth = prolongator.shape[3:]
    whole_map = pl.BlockSpec(memory_space=pltpu.SMEM)
    vmem = pl.BlockSpec(memory_space=pltpu.VMEM)
    one_aggregate = pl.BlockSpec((1, 1, 1, coarse, depth), lambda a: (0, 0, a, 0, 0))
    whole_field = pl.BlockSpec((1, 1, rows, columns), lambda a: (0, 0, 0, 0))
    limit = 48 * 1024 * 1024

    restricted = pl.pallas_call(
        restrict_kernel,
        grid=(SITES,),
        out_shape=jax.ShapeDtypeStruct((coarse, LANES), jnp.float32),
        in_specs=[whole_map, whole_field, one_aggregate],
        out_specs=pl.BlockSpec((coarse, LANES), lambda a: (0, 0)),
        scratch_shapes=[pltpu.VMEM((3, rows, LANES), jnp.float32)],
        compiler_params=pltpu.CompilerParams(vmem_limit_bytes=limit),
    )(site_map, fine_field, prolongator)

    dma = pltpu.SemaphoreType.DMA
    coarse_residual, norm, third = pl.pallas_call(
        functools.partial(richardson_kernel, nz, nt),
        out_shape=(
            jax.ShapeDtypeStruct((1, 1, SITES, coarse, RHS), jnp.float32),
            jax.ShapeDtypeStruct((1, LANES), jnp.float32),
            jax.ShapeDtypeStruct((LANES, coarse), jnp.bfloat16),
        ),
        in_specs=[vmem, vmem],
        out_specs=(vmem, vmem, vmem),
        scratch_shapes=[
            pltpu.VMEM((SITES * coarse, 10 * coarse), jnp.bfloat16),
            pltpu.VMEM((2, coarse, LANES), jnp.bfloat16),
            pltpu.VMEM((2, 4 * coarse, LANES), jnp.bfloat16),
            pltpu.VMEM((2, 8, LANES), jnp.float32),
            pltpu.VMEM((nz - 1, 8, LANES), jnp.float32),
            pltpu.VMEM((nt - 1, 8, LANES), jnp.float32),
            dma((2, 4)),
            dma((2, 4)),
            dma((nz - 1,)),
            dma((nz - 1,)),
            dma((nt - 1,)),
            dma((nt - 1,)),
        ],
        compiler_params=pltpu.CompilerParams(
            collective_id=0, has_side_effects=True, vmem_limit_bytes=limit
        ),
    )(restricted, coarse_op)

    correction = pl.pallas_call(
        lift_kernel,
        grid=(SITES,),
        out_shape=jax.ShapeDtypeStruct(fine_field.shape, fine_field.dtype),
        in_specs=[whole_map, vmem, one_aggregate],
        out_specs=whole_field,
        scratch_shapes=[
            pltpu.VMEM((rows // SITES * 3 + 8, LANES), jnp.float32),
            pltpu.VMEM((rows * 8, LANES), jnp.float32),
        ],
        compiler_params=pltpu.CompilerParams(vmem_limit_bytes=limit),
    )(site_map, third, prolongator)
    return (correction, coarse_residual, norm[0, :RHS])


def solution(mesh):
    placed = (
        P("gx", "ta", None, None),
        P("gx", "ta", None),
        P("gx", "ta", None, None, None),
        P("gx", "ta", None, None, None, None),
    )
    return jax.shard_map(
        functools.partial(local, mesh.shape["gx"], mesh.shape["ta"]),
        mesh=mesh,
        in_specs=placed,
        out_specs=(P("gx", "ta", None, None), P("gx", "ta", None, None, None), P()),
        check_vma=False,
    )
```

time: 132 us -> 65.1 us (0.49)
  Pallas kernels: 0 us -> 60.9 us
  blocking collectives: 39 us -> 0 us
  local copies, waits for them, and re-layouts: 38.6 us -> 3.37 us
  matrix products: 31.8 us -> 0 us
  starting transfers between devices: 14.3 us -> 0 us
  loops' own time: 5.44 us -> 0 us
    pallas_call x0 -> x3, Pallas kernels: none -> 60.9 us  [the longest x1 24.2 us: local(): pl.pallas_call(lift_kernel, grid=(SITES,), out_shape=jax.ShapeDtypeStruct...]
    psum x1 -> x0, blocking collectives: 39 us -> none  [local(): lax.psum(jnp.sum(coarse_residual * coarse_residual, axis=(0, 1, 2, 3)), (...]
    dot_general x28 -> x0, matrix products: 31.8 us -> none  [the longest x8 16.4 us: one_block(): jnp.einsum('ztbk,ztkc->ztbc', table.astype(jnp.bfloat16), values, preferr...]
    ppermute x8 -> x0, starting transfers between devices: 14.3 us -> none  [the longest x4 10.1 us: padded(): lax.ppermute(lax.slice_in_dim(block, 0, width, axis=dim), axis, backward)]
    reshape x1 -> x0, local copies, waits for them, and re-layouts: 13.7 us -> none  [local(): lifted = lifted.reshape(slabs_z, slabs_t, fine_field.shape[2], columns)]
    another operation x3 -> x0, local copies, waits for them, and re-layouts: 11.2 us -> none
    convert_element_type x1 -> x0, local copies, waits for them, and re-layouts: 8.15 us -> none  [local(): lifted = jnp.einsum('ztacm,ztacr->ztamr', prolongator, third_iter, prefer...]
    another operation x2 -> x0, loops' own time: 5.44 us -> none  [permute_rows(): blocks = lax.map(one_block, jnp.arange(count, dtype=jnp.int32))]
  transfers between devices with their start and end apart: 8 -> 0, of which waited for: 2 -> 0; matrix products, arithmetic and copies ran while one was open for 2% -> 0% of each run, Pallas kernels for 0% -> 0%
where the time goes in v1:
time: 65.1 us; the launch traced here: 64.9 us
  Pallas kernels  60.9 us (94%)
  local copies, waits for them, and re-layouts  3.37 us (5%)
  between operations  0.67 us (1%)
    pallas_call x1, Pallas kernels, local(): pl.pallas_call(lift_kernel, grid=(SITES,), out_shape=jax.ShapeDtypeStruct...  24.2 us
    pallas_call x1, Pallas kernels, local(): pl.pallas_call(functools.partial(richardson_kernel, nz, nt), out_shape=(j...  20.7 us
    pallas_call x1, Pallas kernels, local(): pl.pallas_call(restrict_kernel, grid=(SITES,), out_shape=jax.ShapeDtypeSt...  15.9 us
    unnamed x9, local copies, waits for them, and re-layouts  2.85 us

profile of v1, /device:TPU:0, one launch (start us, length us, event | category | flops | bytes accessed | tf_op | source)
XLA Modules:
  0.0 64.9 jit_solution(11988674994719668144)
XLA Ops:
  0.6 0.0 copy-start
  0.6 1.4 %copy-done = bf16[1,1,2048,384]{3,2,1,0:T(8,128)(2,1)S(1)} copy-done((bf16[1,1,2048,384]{3,2,1,0:T(8,128)(2,1)S(1)}, bf16[1,1,2048,384]{3,2,1,0:T(8,128)(2,1)}, u32[]{:S(2)}) %copy-start) | copy-done | bytes 1572888
  2.0 0.0 copy-start.2
  2.0 0.7 %copy-done.2 = s32[1,1,2048]{2,1,0:T(1,128)S(1)} copy-done((s32[1,1,2048]{2,1,0:T(1,128)S(1)}, s32[1,1,2048]{2,1,0:T(1,128)}, u32[]{:S(2)}) %copy-start.2) | copy-done | bytes 8216
  2.7 0.0 copy-start.1
  2.7 0.0 copy-start.3
  2.7 15.9 %shard_map.67.rest_ref = f32[64,128]{1,0:T(8,128)S(1)} custom-call(s32[1,1,2048]{2,1,0:T(1,128)S(1)} %copy-done.2, bf16[1,1,2048,384]{3,2,1,0:T(8,128)(2,1)S(1)} %copy-done, bf16[1,1,8,64,6144]{4,3,2,1,0:T(8,128)(2,1)} %prol_ref.3), custom_call_target="tpu_custom_call" | custom-call | tf_op jit(solution)/shard_map/pallas_call | solution.py:232
  18.7 0.0 copy-done.1
  18.7 20.7 %shard_map.68 = (f32[1,1,8,64,16]{4,3,2,1,0:T(8,128)S(1)}, f32[1,128]{1,0:T(1,128)S(1)}, bf16[128,64]{1,0:T(8,128)(2,1)S(1)}) custom-call(f32[64,128]{1,0:T(8,128)S(1)} %shard_map.67.rest_ref, bf16[1,1,8,9,64,64]{5,4,3,2,1,0:T(8,128)(2,1)S(1)} %copy-done.1), custom_call_target="tpu_custom_call" | custom-call | tf_op jit(solution)/shard_map/pallas_call | solution.py:243
  39.4 0.5 slice_bitcast_fusion
  39.9 0.8 %copy.7 = f32[1,1,8,64,16]{3,4,2,1,0:T(8,128)} copy(f32[1,1,8,64,16]{4,3,2,1,0:T(8,128)S(1)} %get-tuple-element.10) | data formatting | bytes 65536
  40.7 0.0 copy-done.3
  40.7 24.2 %shard_map.69 = bf16[1,1,2048,384]{3,2,1,0:T(8,128)(2,1)} custom-call(s32[1,1,2048]{2,1,0:T(1,128)S(1)} %copy-done.3, bf16[128,64]{1,0:T(8,128)(2,1)S(1)} %get-tuple-element.6.third_ref, bf16[1,1,8,64,6144]{4,3,2,1,0:T(8,128)(2,1)} %prol_ref.3), custom_call_target="tpu_custom_call" | custom-call | tf_op jit(solution)/shard_map/pallas_call | solution.py:271
Async XLA Ops:
  0.6 1.4 %copy-start = (bf16[1,1,2048,384]{3,2,1,0:T(8,128)(2,1)S(1)}, bf16[1,1,2048,384]{3,2,1,0:T(8,128)(2,1)}, u32[]{:S(2)}) copy-start(bf16[1,1,2048,384]{3,2,1,0:T(8,128)(2,1)} %fine_ref.1) | copy-start | bytes 4718596
  2.0 0.7 %copy-start.2 = (s32[1,1,2048]{2,1,0:T(1,128)S(1)}, s32[1,1,2048]{2,1,0:T(1,128)}, u32[]{:S(2)}) copy-start(s32[1,1,2048]{2,1,0:T(1,128)} %map_ref.3) | copy-start | bytes 24580
  2.7 15.9 %copy-start.1 = (bf16[1,1,8,9,64,64]{5,4,3,2,1,0:T(8,128)(2,1)S(1)}, bf16[1,1,8,9,64,64]{5,4,3,2,1,0:T(8,128)(2,1)}, u32[]{:S(2)}) copy-start(bf16[1,1,8,9,64,64]{5,4,3,2,1,0:T(8,128)(2,1)} %op_ref.1) | copy-start | bytes 1769476
  2.7 37.9 %copy-start.3 = (s32[1,1,2048]{2,1,0:T(1,128)S(1)}, s32[1,1,2048]{2,1,0:T(1,128)}, u32[]{:S(2)}) copy-start(s32[1,1,2048]{2,1,0:T(1,128)} %map_ref.3) | copy-start | bytes 24580

commit v2 on v1

v2 whole, which is shorter than its diff:
```python
import functools

import jax
import jax.numpy as jnp
from jax import lax
from jax.experimental import pallas as pl
from jax.experimental.pallas import tpu as pltpu
from jax.sharding import PartitionSpec as P

SPIN = 24
XC = 4
YC = 2
SITES = XC * YC
LANES = 128
RHS = 16
STEP = 32
MESH = pl.DeviceIdType.MESH


def lane_group(shape):
    return lax.broadcasted_iota(jnp.int32, shape, len(shape) - 1) // RHS


def restrict_kernel(
    map_ref, fine_hbm, prol_hbm, rest_ref, inverse_ref, fine, prol, wide, field_sem, prol_sem
):
    rows = fine.shape[0]
    sites = rows // SITES
    coarse = prol.shape[1]
    parts = 4
    size = rows // parts

    def field_copy(n):
        at = pl.ds(n * size, size)
        return pltpu.make_async_copy(fine_hbm.at[0, 0, at], fine.at[at], field_sem.at[n])

    def prol_copy(n):
        return pltpu.make_async_copy(prol_hbm.at[0, 0, n], prol.at[n], prol_sem.at[n])

    for n in range(parts):
        field_copy(n).start()
    for n in range(SITES):
        prol_copy(n).start()
    for n in range(parts):
        field_copy(n).wait()

        def widen(index, carry):
            at = pl.ds(pl.multiple_of(n * size + index * 64, 64), 64)
            for g in range(3):
                wide[g, at, :] = fine[at, g * LANES:(g + 1) * LANES].astype(jnp.float32)
            return carry
        lax.fori_loop(0, size // 64, widen, 0)

    diagonal = lax.broadcasted_iota(jnp.int32, (8, LANES), 0) == lane_group((8, LANES))
    group = lane_group((coarse, LANES))

    def one_aggregate(agg, packed):
        prol_copy(agg).wait()

        def body(chunk, acc):
            parts = []
            for k in range(STEP):
                at = agg * sites + chunk * STEP + k
                row = map_ref[0, 0, at]
                inverse_ref[0, row] = at
                for g in range(3):
                    one = jnp.broadcast_to(wide[g, pl.ds(row, 1), :], (8, LANES))
                    parts.append(jnp.where(diagonal, one, 0.0))
            tiles = [
                jnp.concatenate(parts[i:i + 2], axis=0).astype(jnp.bfloat16)
                for i in range(0, len(parts), 2)
            ]
            spread = jnp.concatenate(tiles, axis=0)
            width = STEP * SPIN
            block = prol[agg, :, pl.ds(pl.multiple_of(chunk * width, width), width)]
            return acc + jnp.dot(block, spread, preferred_element_type=jnp.float32)

        acc = lax.fori_loop(
            0, sites // STEP, body, jnp.zeros((coarse, LANES), jnp.float32), unroll=True
        )
        for shift in (16, 32, 64):
            acc = acc + pltpu.roll(acc, shift, 1)
        acc = acc.astype(jnp.bfloat16).astype(jnp.float32)
        return jnp.where(group == agg, acc, packed)

    rest_ref[...] = lax.fori_loop(
        0, SITES, one_aggregate, jnp.zeros((coarse, LANES), jnp.float32)
    )


def richardson_kernel(
    nz, nt, inverse_ref, rest_ref, op_ref, prol_hbm, out_ref, resid_ref, norm_ref,
    prol, deal, lines, held, placed, packed, sent, halo, part, sums_z, sums_t,
    prol_sem, send_sem, recv_sem, zs_sem, zr_sem, ts_sem, tr_sem,
):
    blocks = [
        pltpu.make_async_copy(prol_hbm.at[0, 0, n], prol.at[n], prol_sem.at[n])
        for n in range(SITES)
    ]
    for copy in blocks:
        copy.start()
    z, t = lax.axis_index("gx"), lax.axis_index("ta")
    barrier = pltpu.get_barrier_semaphore()
    for d in range(1, nz):
        pl.semaphore_signal(barrier, inc=1, device_id=(lax.rem(z + d, nz), t), device_id_type=MESH)
    for d in range(1, nt):
        pl.semaphore_signal(barrier, inc=1, device_id=(z, lax.rem(t + d, nt)), device_id_type=MESH)

    rest = rest_ref[...]
    coarse = rest.shape[0]
    first = 0.5 * rest
    sent[0] = first.astype(jnp.bfloat16)

    targets = (
        (lax.rem(z + nz - 1, nz), t),
        (lax.rem(z + 1, nz), t),
        (z, lax.rem(t + nt - 1, nt)),
        (z, lax.rem(t + 1, nt)),
    )

    def exchange(turn):
        copies = []
        for slot, target in enumerate(targets):
            copy = pltpu.make_async_remote_copy(
                src_ref=sent.at[turn],
                dst_ref=halo.at[turn, pl.ds(slot * coarse, coarse)],
                send_sem=send_sem.at[turn, slot],
                recv_sem=recv_sem.at[turn, slot],
                device_id=target,
                device_id_type=MESH,
            )
            copy.start()
            copies.append(copy)
        return copies

    group = lane_group(rest.shape)
    even = lax.rem(group, 2) == 0

    def pick(full):
        result = full[0:coarse]
        for s in range(1, SITES):
            result = jnp.where(group == s, full[s * coarse:(s + 1) * coarse], result)
        return result

    depth = prol.shape[2]
    rows = out_ref.shape[2]

    line = lax.broadcasted_iota(jnp.int32, (256, 256), 0)
    column = lax.broadcasted_iota(jnp.int32, (256, 256), 1)
    for u in range(4):
        turned = lax.rem(lax.rem(column, LANES) // 32 + (4 - u), 4)
        source = 8 * lax.rem(column, 32) + 4 * (column // LANES) + turned
        deal[u] = (line == source).astype(jnp.float32).astype(jnp.bfloat16)

    def deal_lanes(begin, end):
        def body(index, carry):
            for u in range(4):
                at = pl.ds(pl.multiple_of(index * 1024 + u * 256, 256), 256)
                block = prol[:, :, at].reshape(SITES * coarse, 256)
                moved = jnp.dot(block, deal[u], preferred_element_type=jnp.float32)
                prol[:, :, at] = moved.astype(jnp.bfloat16).reshape(SITES, coarse, 256)
            return carry
        lax.fori_loop(begin, end, body, 0)

    pieces = depth // 1024

    def apply_blocks(values, turn, copies):
        up = pltpu.roll(values, LANES - YC * RHS, 1)
        down = pltpu.roll(values, YC * RHS, 1)
        swap = jnp.where(even, pltpu.roll(values, LANES - RHS, 1), pltpu.roll(values, RHS, 1))
        zero = jnp.zeros_like(values)
        stack = jnp.concatenate([values, up, down, swap, swap, zero], axis=0).astype(jnp.bfloat16)
        full = jnp.dot(packed[:, 4 * coarse:], stack, preferred_element_type=jnp.float32)
        near = pick(full)
        deal_lanes(turn * pieces // 2, (turn + 1) * pieces // 2)
        for copy in copies:
            copy.wait()
        far = jnp.dot(packed[:, :4 * coarse], halo[turn], preferred_element_type=jnp.float32)
        return near + pick(far)

    pl.semaphore_wait(barrier, nz - 1 + nt - 1)
    copies = exchange(0)
    for h in range(9):
        at = (h - 5 if h >= 5 else h + 4) * coarse
        for s in range(SITES):
            packed[s * coarse:(s + 1) * coarse, at:at + coarse] = op_ref[0, 0, s, h]
    for copy in blocks:
        copy.wait()
    packed[:, 9 * coarse:] = jnp.zeros((SITES * coarse, coarse), jnp.bfloat16)
    first_resid = rest - apply_blocks(first, 0, copies)
    second_low = (first + 0.5 * first_resid).astype(jnp.bfloat16)
    sent[1] = second_low
    copies = exchange(1)
    second = second_low.astype(jnp.float32)
    resid = rest - apply_blocks(second, 1, copies)

    total = jnp.sum((resid * resid).reshape(coarse // 8, 8, LANES), axis=0)
    for shift in (16, 32, 64):
        total = total + pltpu.roll(total, shift, 1)
    part[0] = total

    def gather(turn, count, device, sums, s_sem, r_sem):
        pending = []
        for d in range(1, count):
            copy = pltpu.make_async_remote_copy(
                src_ref=part.at[turn],
                dst_ref=sums.at[d - 1],
                send_sem=s_sem.at[d - 1],
                recv_sem=r_sem.at[d - 1],
                device_id=device(d),
                device_id_type=MESH,
            )
            copy.start()
            pending.append(copy)
        return pending

    along_z = gather(0, nz, lambda d: (lax.rem(z + d, nz), t), sums_z, zs_sem, zr_sem)
    third = (second + 0.5 * resid).astype(jnp.bfloat16).astype(jnp.float32)
    lines[...] = jnp.transpose(third).astype(jnp.bfloat16)
    spot = lax.broadcasted_iota(jnp.int32, (RHS, LANES), 1) // 32
    quarter = lax.rem(lane_group((32, LANES)), 4)

    def lift(agg):
        left = lines[pl.ds(pl.multiple_of(agg * RHS, RHS), RHS), :]
        for b in range(pieces):
            flat = jnp.dot(
                left, prol[agg, :, b * 1024:(b + 1) * 1024], preferred_element_type=jnp.float32
            )
            stacked = []
            for i in range(8):
                half = i // 4 * LANES
                piece = flat[:, half:half + LANES]
                for u in range(1, 4):
                    other = flat[:, u * 256 + half:u * 256 + half + LANES]
                    piece = jnp.where(spot == (i + u) % 4, other, piece)
                stacked.append(piece)
            turned = jnp.transpose(jnp.concatenate(stacked, axis=0))
            for u in range(4):
                piece = turned[u * 32:(u + 1) * 32]
                for i in range(1, 4):
                    from_row = (i + u) % 4 * 32
                    piece = jnp.where(quarter == i, turned[from_row:from_row + 32], piece)
                at = agg * (depth // 8) + b * LANES + u * 32
                held[pl.ds(pl.multiple_of(at, 32), 32), :] = piece

    def lift_range(begin, end):
        def body(agg, carry):
            lift(agg)
            return carry
        lax.fori_loop(begin, end, body, 0)

    lift_range(0, SITES // 2)
    for copy in along_z:
        copy.wait()
    for d in range(nz - 1):
        total = total + sums_z[d]
    part[1] = total
    along_t = gather(1, nt, lambda d: (z, lax.rem(t + d, nt)), sums_t, ts_sem, tr_sem)
    for s in range(SITES):
        resid_ref[0, 0, s] = resid[:, s * RHS:(s + 1) * RHS]
    lift_range(SITES // 2, SITES)
    held[pl.ds(3 * rows, 8), :] = jnp.zeros((8, LANES), jnp.float32)

    def place(index, carry):
        for k in range(STEP):
            at = index * STEP + k
            source = inverse_ref[0, at]
            placed[pl.ds(pl.multiple_of(at * 8, 8), 8), :] = held[pl.ds(3 * source, 8), :]
        return carry
    lax.fori_loop(0, rows // STEP, place, 0)

    def narrow(index, carry):
        at = pl.ds(pl.multiple_of(index * 64, 64), 64)
        for g in range(3):
            out_ref[0, 0, at, g * LANES:(g + 1) * LANES] = placed[
                pl.ds(index * 512 + g, 64, stride=8), :
            ].astype(jnp.bfloat16)
        return carry
    lax.fori_loop(0, rows // 64, narrow, 0)
    for copy in along_t:
        copy.wait()
    for d in range(nt - 1):
        total = total + sums_t[d]
    norm_ref[...] = jnp.sqrt(jnp.sum(total, axis=0, keepdims=True) + 1e-06)


def local(nz, nt, fine_field, site_map, prolongator, coarse_op):
    rows, columns = fine_field.shape[2:]
    coarse, depth = prolongator.shape[3:]
    smem = pl.BlockSpec(memory_space=pltpu.SMEM)
    vmem = pl.BlockSpec(memory_space=pltpu.VMEM)
    hbm = pl.BlockSpec(memory_space=pl.ANY)
    dma = pltpu.SemaphoreType.DMA
    limit = 58 * 1024 * 1024

    restricted, inverse = pl.pallas_call(
        restrict_kernel,
        out_shape=(
            jax.ShapeDtypeStruct((coarse, LANES), jnp.float32),
            jax.ShapeDtypeStruct((1, rows), jnp.int32),
        ),
        in_specs=[smem, hbm, hbm],
        out_specs=(vmem, smem),
        scratch_shapes=[
            pltpu.VMEM((rows, columns), jnp.bfloat16),
            pltpu.VMEM((SITES, coarse, depth), jnp.bfloat16),
            pltpu.VMEM((3, rows, LANES), jnp.float32),
            dma((4,)),
            dma((SITES,)),
        ],
        compiler_params=pltpu.CompilerParams(vmem_limit_bytes=limit),
    )(site_map, fine_field, prolongator)

    correction, coarse_residual, norm = pl.pallas_call(
        functools.partial(richardson_kernel, nz, nt),
        out_shape=(
            jax.ShapeDtypeStruct(fine_field.shape, fine_field.dtype),
            jax.ShapeDtypeStruct((1, 1, SITES, coarse, RHS), jnp.float32),
            jax.ShapeDtypeStruct((1, LANES), jnp.float32),
        ),
        in_specs=[smem, vmem, vmem, hbm],
        out_specs=(vmem, vmem, vmem),
        scratch_shapes=[
            pltpu.VMEM((SITES, coarse, depth), jnp.bfloat16),
            pltpu.VMEM((4, 256, 256), jnp.bfloat16),
            pltpu.VMEM((LANES, coarse), jnp.bfloat16),
            pltpu.VMEM((rows * 3 + 8, LANES), jnp.float32),
            pltpu.VMEM((rows * 8, LANES), jnp.float32),
            pltpu.VMEM((SITES * coarse, 10 * coarse), jnp.bfloat16),
            pltpu.VMEM((2, coarse, LANES), jnp.bfloat16),
            pltpu.VMEM((2, 4 * coarse, LANES), jnp.bfloat16),
            pltpu.VMEM((2, 8, LANES), jnp.float32),
            pltpu.VMEM((nz - 1, 8, LANES), jnp.float32),
            pltpu.VMEM((nt - 1, 8, LANES), jnp.float32),
            dma((SITES,)),
            dma((2, 4)),
            dma((2, 4)),
            dma((nz - 1,)),
            dma((nz - 1,)),
            dma((nt - 1,)),
            dma((nt - 1,)),
        ],
        compiler_params=pltpu.CompilerParams(
            collective_id=0, has_side_effects=True, vmem_limit_bytes=limit
        ),
    )(inverse, restricted, coarse_op, prolongator)
    return (correction, coarse_residual, norm[0, :RHS])


def solution(mesh):
    placed = (
        P("gx", "ta", None, None),
        P("gx", "ta", None),
        P("gx", "ta", None, None, None),
        P("gx", "ta", None, None, None, None),
    )
    return jax.shard_map(
        functools.partial(local, mesh.shape["gx"], mesh.shape["ta"]),
        mesh=mesh,
        in_specs=placed,
        out_specs=(P("gx", "ta", None, None), P("gx", "ta", None, None, None), P()),
        check_vma=False,
    )
```

time: 65.1 us -> 44.8 us (0.69)
  Pallas kernels: 60.9 us -> 38.3 us
  local copies, waits for them, and re-layouts: 3.37 us -> 5.6 us
    pallas_call x2 -> x1, Pallas kernels: 40.1 us -> 12.6 us  [local(): pl.pallas_call(restrict_kernel, out_shape=(jax.ShapeDtypeStruct((coarse,...]
    pallas_call x1, Pallas kernels: 20.7 us -> 25.7 us  [local(): pl.pallas_call(functools.partial(richardson_kernel, nz, nt), out_shape=(j...]
    unnamed x9 -> x2, local copies, waits for them, and re-layouts: 2.85 us -> 4.41 us
    squeeze x1, local copies, waits for them, and re-layouts: 0.51 us -> 1.19 us  [local(): return (correction, coarse_residual, norm[0, :RHS])]
where the time goes in v2:
time: 44.8 us; the launch traced here: 44.6 us
  Pallas kernels  38.3 us (85%)
  local copies, waits for them, and re-layouts  5.6 us (12%)
  between operations  0.65 us (1%)
    pallas_call x1, Pallas kernels, local(): pl.pallas_call(functools.partial(richardson_kernel, nz, nt), out_shape=(j...  25.7 us
    pallas_call x1, Pallas kernels, local(): pl.pallas_call(restrict_kernel, out_shape=(jax.ShapeDtypeStruct((coarse,...  12.6 us
    unnamed x2, local copies, waits for them, and re-layouts  4.41 us
    squeeze x1, local copies, waits for them, and re-layouts, local(): return (correction, coarse_residual, norm[0, :RHS])  1.19 us

profile of v2, /device:TPU:0, one launch (start us, length us, event | category | flops | bytes accessed | tf_op | source)
XLA Modules:
  0.0 44.6 jit_solution(12391708388048692597)
XLA Ops:
  0.6 12.6 %shard_map.67 = (f32[64,128]{1,0:T(8,128)}, s32[1,2048]{1,0:T(1,128)}) custom-call(s32[1,1,2048]{2,1,0:T(1,128)} %map_ref.1, bf16[1,1,2048,384]{3,2,1,0:T(8,128)(2,1)} %fine_hbm.1, bf16[1,1,8,64,6144]{4,3,2,1,0:T(8,128)(2,1)} %prol_hbm.3), custom_call_target="tpu_custom_call" | custom-call | tf_op jit(solution)/shard_map/pallas_call | solution.py:296
  13.2 25.7 %shard_map.68 = (bf16[1,1,2048,384]{3,2,1,0:T(8,128)(2,1)}, f32[1,1,8,64,16]{4,3,2,1,0:T(8,128)}, f32[1,128]{1,0:T(1,128)}) custom-call(s32[1,2048]{1,0:T(1,128)} %get-tuple-element.8.inverse_ref, f32[64,128]{1,0:T(8,128)} %get-tuple-element.9.rest_ref, bf16[1,1,8,9,64,64]{5,4,3,2,1,0:T(8,128)(2,1)} %op_ref.1, bf16[1,1,8,64,6144]{4,3,2,1,0:T(8,128)(2,1)} %prol_hbm.3), custom_call_target="tpu_custom_call" | custom-call | tf_op jit(solution)/shard_map/pallas_call | solution.py:314
  39.0 1.2 %slice_bitcast_fusion = f32[16]{0:T(128)} fusion(f32[1,128]{1,0:T(1,128)} %get-tuple-element.12), kind=kLoop, calls=%fused_computation | loop fusion | bytes 128 | tf_op jit(solution)/shard_map/squeeze | solution.py:347
  40.2 1.7 %copy.7 = f32[1,1,8,64,16]{3,4,2,1,0:T(8,128)} copy(f32[1,1,8,64,16]{4,3,2,1,0:T(8,128)} %get-tuple-element.14) | data formatting | bytes 65536
  41.9 2.7 %copy.9 = bf16[1,1,2048,384]{3,2,1,0:T(8,128)(2,1)} copy(bf16[1,1,2048,384]{3,2,1,0:T(8,128)(2,1)} %get-tuple-element.19) | data formatting | bytes 3145728

commit v3 on v2

--- a/solution.py
+++ b/solution.py
@@ -22,7 +22,7 @@
 
 
 def restrict_kernel(
-    map_ref, fine_hbm, prol_hbm, rest_ref, inverse_ref, fine, prol, wide, field_sem, prol_sem
+    map_ref, fine_hbm, prol_hbm, rest_ref, prol, fine, wide, field_sem, prol_sem
 ):
     rows = fine.shape[0]
     sites = rows // SITES
@@ -60,9 +60,7 @@
         def body(chunk, acc):
             parts = []
             for k in range(STEP):
-                at = agg * sites + chunk * STEP + k
-                row = map_ref[0, 0, at]
-                inverse_ref[0, row] = at
+                row = map_ref[0, 0, agg * sites + chunk * STEP + k]
                 for g in range(3):
                     one = jnp.broadcast_to(wide[g, pl.ds(row, 1), :], (8, LANES))
                     parts.append(jnp.where(diagonal, one, 0.0))
@@ -89,16 +87,10 @@
 
 
 def richardson_kernel(
-    nz, nt, inverse_ref, rest_ref, op_ref, prol_hbm, out_ref, resid_ref, norm_ref,
-    prol, deal, lines, held, placed, packed, sent, halo, part, sums_z, sums_t,
-    prol_sem, send_sem, recv_sem, zs_sem, zr_sem, ts_sem, tr_sem,
+    nz, nt, rest_ref, op_ref, source, held, resid_ref, norm_ref,
+    prol, deal, lines, packed, sent, halo, part, sums_z, sums_t,
+    send_sem, recv_sem, zs_sem, zr_sem, ts_sem, tr_sem,
 ):
-    blocks = [
-        pltpu.make_async_copy(prol_hbm.at[0, 0, n], prol.at[n], prol_sem.at[n])
-        for n in range(SITES)
-    ]
-    for copy in blocks:
-        copy.start()
     z, t = lax.axis_index("gx"), lax.axis_index("ta")
     barrier = pltpu.get_barrier_semaphore()
     for d in range(1, nz):
@@ -143,20 +135,19 @@
         return result
 
     depth = prol.shape[2]
-    rows = out_ref.shape[2]
 
     line = lax.broadcasted_iota(jnp.int32, (256, 256), 0)
     column = lax.broadcasted_iota(jnp.int32, (256, 256), 1)
     for u in range(4):
         turned = lax.rem(lax.rem(column, LANES) // 32 + (4 - u), 4)
-        source = 8 * lax.rem(column, 32) + 4 * (column // LANES) + turned
-        deal[u] = (line == source).astype(jnp.float32).astype(jnp.bfloat16)
+        origin = 8 * lax.rem(column, 32) + 4 * (column // LANES) + turned
+        deal[u] = (line == origin).astype(jnp.float32).astype(jnp.bfloat16)
 
     def deal_lanes(begin, end):
         def body(index, carry):
             for u in range(4):
                 at = pl.ds(pl.multiple_of(index * 1024 + u * 256, 256), 256)
-                block = prol[:, :, at].reshape(SITES * coarse, 256)
+                block = source[:, :, at].reshape(SITES * coarse, 256)
                 moved = jnp.dot(block, deal[u], preferred_element_type=jnp.float32)
                 prol[:, :, at] = moved.astype(jnp.bfloat16).reshape(SITES, coarse, 256)
             return carry
@@ -184,8 +175,6 @@
         at = (h - 5 if h >= 5 else h + 4) * coarse
         for s in range(SITES):
             packed[s * coarse:(s + 1) * coarse, at:at + coarse] = op_ref[0, 0, s, h]
-    for copy in blocks:
-        copy.wait()
     packed[:, 9 * coarse:] = jnp.zeros((SITES * coarse, coarse), jnp.bfloat16)
     first_resid = rest - apply_blocks(first, 0, copies)
     second_low = (first + 0.5 * first_resid).astype(jnp.bfloat16)
@@ -249,6 +238,7 @@
             return carry
         lax.fori_loop(begin, end, body, 0)
 
+    held[pl.ds(SITES * depth // 8, 8), :] = jnp.zeros((8, LANES), jnp.float32)
     lift_range(0, SITES // 2)
     for copy in along_z:
         copy.wait()
@@ -256,27 +246,8 @@
         total = total + sums_z[d]
     part[1] = total
     along_t = gather(1, nt, lambda d: (z, lax.rem(t + d, nt)), sums_t, ts_sem, tr_sem)
-    for s in range(SITES):
-        resid_ref[0, 0, s] = resid[:, s * RHS:(s + 1) * RHS]
     lift_range(SITES // 2, SITES)
-    held[pl.ds(3 * rows, 8), :] = jnp.zeros((8, LANES), jnp.float32)
-
-    def place(index, carry):
-        for k in range(STEP):
-            at = index * STEP + k
-            source = inverse_ref[0, at]
-            placed[pl.ds(pl.multiple_of(at * 8, 8), 8), :] = held[pl.ds(3 * source, 8), :]
-        return carry
-    lax.fori_loop(0, rows // STEP, place, 0)
-
-    def narrow(index, carry):
-        at = pl.ds(pl.multiple_of(index * 64, 64), 64)
-        for g in range(3):
-            out_ref[0, 0, at, g * LANES:(g + 1) * LANES] = placed[
-                pl.ds(index * 512 + g, 64, stride=8), :
-            ].astype(jnp.bfloat16)
-        return carry
-    lax.fori_loop(0, rows // 64, narrow, 0)
+    resid_ref[...] = jnp.transpose(resid)
     for copy in along_t:
         copy.wait()
     for d in range(nt - 1):
@@ -284,55 +255,85 @@
     norm_ref[...] = jnp.sqrt(jnp.sum(total, axis=0, keepdims=True) + 1e-06)
 
 
+def place_kernel(
+    map_ref, held, resid, norm, out_hbm, resid_ref, norm_ref, placed, out, out_sem
+):
+    rows = out.shape[0]
+    norm_ref[...] = norm[:, :RHS]
+    resid_ref[0, 0] = resid[...].reshape(resid_ref.shape[2:])
+
+    def place(index, carry):
+        for k in range(STEP):
+            at = index * STEP + k
+            row = map_ref[0, 0, at]
+            placed[pl.ds(pl.multiple_of(row * 8, 8), 8), :] = held[pl.ds(3 * at, 8), :]
+        return carry
+    lax.fori_loop(0, rows // STEP, place, 0)
+
+    def copy_out(n):
+        at = pl.ds(pl.multiple_of(n * 256, 256), 256)
+        return pltpu.make_async_copy(out.at[at], out_hbm.at[0, 0, at], out_sem.at[n])
+
+    def narrow(index, carry):
+        for g in range(3):
+            out[pl.ds(pl.multiple_of(index * 256, 256), 256), g * LANES:(g + 1) * LANES] = (
+                placed[pl.ds(index * 2048 + g, 256, stride=8), :].astype(jnp.bfloat16)
+            )
+        copy_out(index).start()
+        return carry
+    lax.fori_loop(0, rows // 256, narrow, 0)
+
+    def finish(index, carry):
+        copy_out(index).wait()
+        return carry
+    lax.fori_loop(0, rows // 256, finish, 0)
+
+
 def local(nz, nt, fine_field, site_map, prolongator, coarse_op):
     rows, columns = fine_field.shape[2:]
     coarse, depth = prolongator.shape[3:]
     smem = pl.BlockSpec(memory_space=pltpu.SMEM)
     vmem = pl.BlockSpec(memory_space=pltpu.VMEM)
-    hbm = pl.BlockSpec(memory_space=pl.ANY)
+    hbm = pl.BlockSpec(memory_space=pltpu.HBM)
     dma = pltpu.SemaphoreType.DMA
-    limit = 58 * 1024 * 1024
-
-    restricted, inverse = pl.pallas_call(
+    limit = 36 * 1024 * 1024
+
+    restricted, held_prolongator = pl.pallas_call(
         restrict_kernel,
         out_shape=(
-            jax.ShapeDtypeStruct((coarse, LANES), jnp.float32),
-            jax.ShapeDtypeStruct((1, rows), jnp.int32),
+            pltpu.VMEM((coarse, LANES), jnp.float32),
+            pltpu.VMEM((SITES, coarse, depth), jnp.bfloat16),
         ),
         in_specs=[smem, hbm, hbm],
-        out_specs=(vmem, smem),
+        out_specs=(vmem, vmem),
         scratch_shapes=[
             pltpu.VMEM((rows, columns), jnp.bfloat16),
-            pltpu.VMEM((SITES, coarse, depth), jnp.bfloat16),
             pltpu.VMEM((3, rows, LANES), jnp.float32),
             dma((4,)),
             dma((SITES,)),
         ],
-        compiler_params=pltpu.CompilerParams(vmem_limit_bytes=limit),
+        compiler_params=pltpu.CompilerParams(vmem_limit_bytes=57 * 1024 * 1024),
     )(site_map, fine_field, prolongator)
 
-    correction, coarse_residual, norm = pl.pallas_call(
+    held, packed_residual, norm = pl.pallas_call(
         functools.partial(richardson_kernel, nz, nt),
         out_shape=(
-            jax.ShapeDtypeStruct(fine_field.shape, fine_field.dtype),
-            jax.ShapeDtypeStruct((1, 1, SITES, coarse, RHS), jnp.float32),
-            jax.ShapeDtypeStruct((1, LANES), jnp.float32),
+            pltpu.VMEM((rows * 3 + 8, LANES), jnp.float32),
+            pltpu.VMEM((LANES, coarse), jnp.float32),
+            pltpu.VMEM((1, LANES), jnp.float32),
         ),
-        in_specs=[smem, vmem, vmem, hbm],
+        in_specs=[vmem, vmem, vmem],
         out_specs=(vmem, vmem, vmem),
         scratch_shapes=[
             pltpu.VMEM((SITES, coarse, depth), jnp.bfloat16),
             pltpu.VMEM((4, 256, 256), jnp.bfloat16),
             pltpu.VMEM((LANES, coarse), jnp.bfloat16),
-            pltpu.VMEM((rows * 3 + 8, LANES), jnp.float32),
-            pltpu.VMEM((rows * 8, LANES), jnp.float32),
             pltpu.VMEM((SITES * coarse, 10 * coarse), jnp.bfloat16),
             pltpu.VMEM((2, coarse, LANES), jnp.bfloat16),
             pltpu.VMEM((2, 4 * coarse, LANES), jnp.bfloat16),
             pltpu.VMEM((2, 8, LANES), jnp.float32),
             pltpu.VMEM((nz - 1, 8, LANES), jnp.float32),
             pltpu.VMEM((nt - 1, 8, LANES), jnp.float32),
-            dma((SITES,)),
             dma((2, 4)),
             dma((2, 4)),
             dma((nz - 1,)),
@@ -343,8 +344,25 @@
         compiler_params=pltpu.CompilerParams(
             collective_id=0, has_side_effects=True, vmem_limit_bytes=limit
         ),
-    )(inverse, restricted, coarse_op, prolongator)
-    return (correction, coarse_residual, norm[0, :RHS])
+    )(restricted, coarse_op, held_prolongator)
+
+    correction, coarse_residual, norm = pl.pallas_call(
+        place_kernel,
+        out_shape=(
+            jax.ShapeDtypeStruct(fine_field.shape, fine_field.dtype),
+            jax.ShapeDtypeStruct((1, 1, SITES, RHS, coarse), jnp.float32),
+            jax.ShapeDtypeStruct((1, RHS), jnp.float32),
+        ),
+        in_specs=[smem, vmem, vmem, vmem],
+        out_specs=(hbm, vmem, vmem),
+        scratch_shapes=[
+            pltpu.VMEM((rows * 8, LANES), jnp.float32),
+            pltpu.VMEM((rows, columns), jnp.bfloat16),
+            dma((rows // 256,)),
+        ],
+        compiler_params=pltpu.CompilerParams(vmem_limit_bytes=limit),
+    )(site_map, held, packed_residual, norm)
+    return (correction, jnp.swapaxes(coarse_residual, 3, 4), norm.reshape(RHS))
 
 
 def solution(mesh):

time: 44.8 us -> 39.3 us (0.88)
  local copies, waits for them, and re-layouts: 5.6 us -> 1.27 us
  Pallas kernels: 38.3 us -> 37.2 us
    unnamed x2 -> x4, local copies, waits for them, and re-layouts: 4.41 us -> 1.27 us
    squeeze x1 -> x0, local copies, waits for them, and re-layouts: 1.19 us -> none  [local(): return (correction, coarse_residual, norm[0, :RHS])]
    pallas_call x2 -> x3, Pallas kernels: 38.3 us -> 37.2 us  [the longest x1 20.6 us: local(): pl.pallas_call(functools.partial(richardson_kernel, nz, nt), out_shape=(p...]
where the time goes in v3:
time: 39.3 us; the launch traced here: 39.1 us
  Pallas kernels  37.2 us (95%)
  local copies, waits for them, and re-layouts  1.27 us (3%)
  between operations  0.66 us (2%)
    pallas_call x1, Pallas kernels, local(): pl.pallas_call(functools.partial(richardson_kernel, nz, nt), out_shape=(p...  20.6 us
    pallas_call x1, Pallas kernels, local(): pl.pallas_call(restrict_kernel, out_shape=(pltpu.VMEM((coarse, LANES), jn...  11.3 us
    pallas_call x1, Pallas kernels, local(): pl.pallas_call(place_kernel, out_shape=(jax.ShapeDtypeStruct(fine_field.s...  5.19 us
    unnamed x4, local copies, waits for them, and re-layouts  1.27 us

profile of v3, /device:TPU:0, one launch (start us, length us, event | category | flops | bytes accessed | tf_op | source)
XLA Modules:
  0.0 39.1 jit_solution(16505003523249435371)
XLA Ops:
  0.6 11.3 %shard_map.67 = (f32[64,128]{1,0:T(8,128)S(1)}, bf16[8,64,6144]{2,1,0:T(8,128)(2,1)S(1)}) custom-call(s32[1,1,2048]{2,1,0:T(1,128)} %map_ref.3, bf16[1,1,2048,384]{3,2,1,0:T(8,128)(2,1)} %fine_hbm.1, bf16[1,1,8,64,6144]{4,3,2,1,0:T(8,128)(2,1)} %prol_hbm.1), custom_call_target="tpu_custom_call" | custom-call | tf_op jit(solution)/shard_map/pallas_call | solution.py:301
  12.0 0.0 copy-start
  12.0 1.3 %copy-done = bf16[1,1,8,9,64,64]{5,4,3,2,1,0:T(8,128)(2,1)S(1)} copy-done((bf16[1,1,8,9,64,64]{5,4,3,2,1,0:T(8,128)(2,1)S(1)}, bf16[1,1,8,9,64,64]{5,4,3,2,1,0:T(8,128)(2,1)}, u32[]{:S(2)}) %copy-start) | copy-done | bytes 589848
  13.2 0.0 copy-start.1
  13.2 20.6 %shard_map.68 = (f32[6152,128]{1,0:T(8,128)S(1)}, f32[128,64]{1,0:T(8,128)S(1)}, f32[1,128]{1,0:T(1,128)S(1)}) custom-call(f32[64,128]{1,0:T(8,128)S(1)} %get-tuple-element.11.rest_ref, bf16[1,1,8,9,64,64]{5,4,3,2,1,0:T(8,128)(2,1)S(1)} %copy-done, bf16[8,64,6144]{2,1,0:T(8,128)(2,1)S(1)} %get-tuple-element.12.source), custom_call_target="tpu_custom_call" | custom-call | tf_op jit(solution)/shard_map/pallas_call | solution.py:318
  33.9 0.0 copy-done.1
  33.9 5.2 %shard_map.69 = (bf16[1,1,2048,384]{3,2,1,0:T(8,128)(2,1)}, f32[1,1,8,16,64]{4,3,2,1,0:T(8,128)}, f32[1,16]{1,0:T(1,128)}) custom-call(s32[1,1,2048]{2,1,0:T(1,128)S(1)} %copy-done.1, f32[6152,128]{1,0:T(8,128)S(1)} %get-tuple-element.13.held, f32[128,64]{1,0:T(8,128)S(1)} %get-tuple-element.14.resid, f32[1,128]{1,0:T(1,128)S(1)} %get-tuple-element.15.norm), custom_call_target="tpu_custom_call" | custom-call | tf_op jit(solution)/shard_map/pallas_call | solution.py:349
Async XLA Ops:
  12.0 1.3 %copy-start = (bf16[1,1,8,9,64,64]{5,4,3,2,1,0:T(8,128)(2,1)S(1)}, bf16[1,1,8,9,64,64]{5,4,3,2,1,0:T(8,128)(2,1)}, u32[]{:S(2)}) copy-start(bf16[1,1,8,9,64,64]{5,4,3,2,1,0:T(8,128)(2,1)} %op_ref.1) | copy-start | bytes 1769476
  13.2 20.7 %copy-start.1 = (s32[1,1,2048]{2,1,0:T(1,128)S(1)}, s32[1,1,2048]{2,1,0:T(1,128)}, u32[]{:S(2)}) copy-start(s32[1,1,2048]{2,1,0:T(1,128)} %map_ref.3) | copy-start | bytes 24580

commit v4 on v3

--- a/solution.py
+++ b/solution.py
@@ -22,7 +22,8 @@
 
 
 def restrict_kernel(
-    map_ref, fine_hbm, prol_hbm, rest_ref, prol, fine, wide, field_sem, prol_sem
+    map_ref, fine_hbm, prol_hbm, op_hbm, rest_ref, prol, op, fine, wide, sums,
+    field_sem, prol_sem, op_sem
 ):
     rows = fine.shape[0]
     sites = rows // SITES
@@ -41,6 +42,8 @@
         field_copy(n).start()
     for n in range(SITES):
         prol_copy(n).start()
+    op_copy = pltpu.make_async_copy(op_hbm, op, op_sem)
+    op_copy.start()
     for n in range(parts):
         field_copy(n).wait()
 
@@ -54,7 +57,7 @@
     diagonal = lax.broadcasted_iota(jnp.int32, (8, LANES), 0) == lane_group((8, LANES))
     group = lane_group((coarse, LANES))
 
-    def one_aggregate(agg, packed):
+    def one_aggregate(agg, carry):
         prol_copy(agg).wait()
 
         def body(chunk, acc):
@@ -73,17 +76,20 @@
             block = prol[agg, :, pl.ds(pl.multiple_of(chunk * width, width), width)]
             return acc + jnp.dot(block, spread, preferred_element_type=jnp.float32)
 
-        acc = lax.fori_loop(
+        sums[agg] = lax.fori_loop(
             0, sites // STEP, body, jnp.zeros((coarse, LANES), jnp.float32), unroll=True
         )
+        return carry
+
+    lax.fori_loop(0, SITES, one_aggregate, 0)
+    packed = jnp.zeros((coarse, LANES), jnp.float32)
+    for agg in range(SITES):
+        acc = sums[agg]
         for shift in (16, 32, 64):
             acc = acc + pltpu.roll(acc, shift, 1)
-        acc = acc.astype(jnp.bfloat16).astype(jnp.float32)
-        return jnp.where(group == agg, acc, packed)
-
-    rest_ref[...] = lax.fori_loop(
-        0, SITES, one_aggregate, jnp.zeros((coarse, LANES), jnp.float32)
-    )
+        packed = jnp.where(group == agg, acc, packed)
+    rest_ref[...] = packed.astype(jnp.bfloat16).astype(jnp.float32)
+    op_copy.wait()
 
 
 def richardson_kernel(
@@ -169,13 +175,13 @@
         far = jnp.dot(packed[:, :4 * coarse], halo[turn], preferred_element_type=jnp.float32)
         return near + pick(far)
 
-    pl.semaphore_wait(barrier, nz - 1 + nt - 1)
-    copies = exchange(0)
     for h in range(9):
         at = (h - 5 if h >= 5 else h + 4) * coarse
         for s in range(SITES):
             packed[s * coarse:(s + 1) * coarse, at:at + coarse] = op_ref[0, 0, s, h]
     packed[:, 9 * coarse:] = jnp.zeros((SITES * coarse, coarse), jnp.bfloat16)
+    pl.semaphore_wait(barrier, nz - 1 + nt - 1)
+    copies = exchange(0)
     first_resid = rest - apply_blocks(first, 0, copies)
     second_low = (first + 0.5 * first_resid).astype(jnp.bfloat16)
     sent[1] = second_low
@@ -236,7 +242,7 @@
         def body(agg, carry):
             lift(agg)
             return carry
-        lax.fori_loop(begin, end, body, 0)
+        lax.fori_loop(begin, end, body, 0, unroll=2)
 
     held[pl.ds(SITES * depth // 8, 8), :] = jnp.zeros((8, LANES), jnp.float32)
     lift_range(0, SITES // 2)
@@ -298,22 +304,25 @@
     dma = pltpu.SemaphoreType.DMA
     limit = 36 * 1024 * 1024
 
-    restricted, held_prolongator = pl.pallas_call(
+    restricted, held_prolongator, held_op = pl.pallas_call(
         restrict_kernel,
         out_shape=(
             pltpu.VMEM((coarse, LANES), jnp.float32),
             pltpu.VMEM((SITES, coarse, depth), jnp.bfloat16),
+            pltpu.VMEM(coarse_op.shape, jnp.bfloat16),
         ),
-        in_specs=[smem, hbm, hbm],
-        out_specs=(vmem, vmem),
+        in_specs=[smem, hbm, hbm, hbm],
+        out_specs=(vmem, vmem, vmem),
         scratch_shapes=[
             pltpu.VMEM((rows, columns), jnp.bfloat16),
             pltpu.VMEM((3, rows, LANES), jnp.float32),
+            pltpu.VMEM((SITES, coarse, LANES), jnp.float32),
             dma((4,)),
             dma((SITES,)),
+            dma(()),
         ],
-        compiler_params=pltpu.CompilerParams(vmem_limit_bytes=57 * 1024 * 1024),
-    )(site_map, fine_field, prolongator)
+        compiler_params=pltpu.CompilerParams(vmem_limit_bytes=56 * 1024 * 1024),
+    )(site_map, fine_field, prolongator, coarse_op)
 
     held, packed_residual, norm = pl.pallas_call(
         functools.partial(richardson_kernel, nz, nt),
@@ -344,7 +353,7 @@
         compiler_params=pltpu.CompilerParams(
             collective_id=0, has_side_effects=True, vmem_limit_bytes=limit
         ),
-    )(restricted, coarse_op, held_prolongator)
+    )(restricted, held_op, held_prolongator)
 
     correction, coarse_residual, norm = pl.pallas_call(
         place_kernel,

time: 39.3 us -> 36.9 us (0.939)
  local copies, waits for them, and re-layouts: 1.27 us -> 0.01 us
  Pallas kernels: 37.2 us -> 36 us
    pallas_call x1, Pallas kernels: 11.3 us -> 10.1 us  [local(): pl.pallas_call(restrict_kernel, out_shape=(pltpu.VMEM((coarse, LANES), jn...]
    unnamed x4 -> x2, local copies, waits for them, and re-layouts: 1.27 us -> 0.01 us
where the time goes in v4:
time: 36.9 us; the launch traced here: 36.7 us
  Pallas kernels  36 us (98%)
  between operations  0.66 us (2%)
    pallas_call x1, Pallas kernels, local(): pl.pallas_call(functools.partial(richardson_kernel, nz, nt), out_shape=(p...  20.7 us
    pallas_call x1, Pallas kernels, local(): pl.pallas_call(restrict_kernel, out_shape=(pltpu.VMEM((coarse, LANES), jn...  10.1 us
    pallas_call x1, Pallas kernels, local(): pl.pallas_call(place_kernel, out_shape=(jax.ShapeDtypeStruct(fine_field.s...  5.19 us

profile of v4, /device:TPU:0, one launch (start us, length us, event | category | flops | bytes accessed | tf_op | source)
XLA Modules:
  0.0 36.7 jit_solution(16173358312274255997)
XLA Ops:
  0.6 10.1 %shard_map.67 = (f32[64,128]{1,0:T(8,128)S(1)}, bf16[8,64,6144]{2,1,0:T(8,128)(2,1)S(1)}, bf16[1,1,8,9,64,64]{5,4,3,2,1,0:T(8,128)(2,1)S(1)}) custom-call(s32[1,1,2048]{2,1,0:T(1,128)} %map_ref.3, bf16[1,1,2048,384]{3,2,1,0:T(8,128)(2,1)} %fine_hbm.1, bf16[1,1,8,64,6144]{4,3,2,1,0:T(8,128)(2,1)} %prol_hbm.1, bf16[1,1,8,9,64,64]{5,4,3,2,1,0:T(8,128)(2,1)} %op_hbm.1), custom_call_target="tpu_custom_call" | custom-call | tf_op jit(solution)/shard_map/pallas_call | solution.py:307
  10.7 0.0 copy-start
  10.7 20.7 %shard_map.68 = (f32[6152,128]{1,0:T(8,128)S(1)}, f32[128,64]{1,0:T(8,128)S(1)}, f32[1,128]{1,0:T(1,128)S(1)}) custom-call(f32[64,128]{1,0:T(8,128)S(1)} %get-tuple-element.12.rest_ref, bf16[1,1,8,9,64,64]{5,4,3,2,1,0:T(8,128)(2,1)S(1)} %get-tuple-element.13.op_ref, bf16[8,64,6144]{2,1,0:T(8,128)(2,1)S(1)} %get-tuple-element.14.source), custom_call_target="tpu_custom_call" | custom-call | tf_op jit(solution)/shard_map/pallas_call | solution.py:327
  31.5 0.0 copy-done
  31.5 5.2 %shard_map.69 = (bf16[1,1,2048,384]{3,2,1,0:T(8,128)(2,1)}, f32[1,1,8,16,64]{4,3,2,1,0:T(8,128)}, f32[1,16]{1,0:T(1,128)}) custom-call(s32[1,1,2048]{2,1,0:T(1,128)S(1)} %copy-done, f32[6152,128]{1,0:T(8,128)S(1)} %get-tuple-element.15.held, f32[128,64]{1,0:T(8,128)S(1)} %get-tuple-element.16.resid, f32[1,128]{1,0:T(1,128)S(1)} %get-tuple-element.17.norm), custom_call_target="tpu_custom_call" | custom-call | tf_op jit(solution)/shard_map/pallas_call | solution.py:358
Async XLA Ops:
  10.7 20.8 %copy-start = (s32[1,1,2048]{2,1,0:T(1,128)S(1)}, s32[1,1,2048]{2,1,0:T(1,128)}, u32[]{:S(2)}) copy-start(s32[1,1,2048]{2,1,0:T(1,128)} %map_ref.3) | copy-start | bytes 24580

commit v5 on v4

--- a/solution.py
+++ b/solution.py
@@ -169,7 +169,8 @@
         stack = jnp.concatenate([values, up, down, swap, swap, zero], axis=0).astype(jnp.bfloat16)
         full = jnp.dot(packed[:, 4 * coarse:], stack, preferred_element_type=jnp.float32)
         near = pick(full)
-        deal_lanes(turn * pieces // 2, (turn + 1) * pieces // 2)
+        if turn == 0:
+            deal_lanes(0, pieces // 2)
         for copy in copies:
             copy.wait()
         far = jnp.dot(packed[:, :4 * coarse], halo[turn], preferred_element_type=jnp.float32)
@@ -245,14 +246,14 @@
         lax.fori_loop(begin, end, body, 0, unroll=2)
 
     held[pl.ds(SITES * depth // 8, 8), :] = jnp.zeros((8, LANES), jnp.float32)
-    lift_range(0, SITES // 2)
+    deal_lanes(pieces // 2, pieces)
     for copy in along_z:
         copy.wait()
     for d in range(nz - 1):
         total = total + sums_z[d]
     part[1] = total
     along_t = gather(1, nt, lambda d: (z, lax.rem(t + d, nt)), sums_t, ts_sem, tr_sem)
-    lift_range(SITES // 2, SITES)
+    lift_range(0, SITES)
     resid_ref[...] = jnp.transpose(resid)
     for copy in along_t:
         copy.wait()

time: 36.9 us -> 36.9 us (level)
  no operation moved by 1% of the time
where the time goes in v5:
time: 36.9 us; the launch traced here: 36.7 us
  Pallas kernels  36.1 us (98%)
  between operations  0.66 us (2%)
    pallas_call x1, Pallas kernels, local(): pl.pallas_call(functools.partial(richardson_kernel, nz, nt), out_shape=(p...  20.8 us
    pallas_call x1, Pallas kernels, local(): pl.pallas_call(restrict_kernel, out_shape=(pltpu.VMEM((coarse, LANES), jn...  10.1 us
    pallas_call x1, Pallas kernels, local(): pl.pallas_call(place_kernel, out_shape=(jax.ShapeDtypeStruct(fine_field.s...  5.19 us

profile of v5, /device:TPU:0, one launch (start us, length us, event | category | flops | bytes accessed | tf_op | source)
XLA Modules:
  0.0 36.7 jit_solution(6920685716728787566)
XLA Ops:
  0.6 10.1 %shard_map.67 = (f32[64,128]{1,0:T(8,128)S(1)}, bf16[8,64,6144]{2,1,0:T(8,128)(2,1)S(1)}, bf16[1,1,8,9,64,64]{5,4,3,2,1,0:T(8,128)(2,1)S(1)}) custom-call(s32[1,1,2048]{2,1,0:T(1,128)} %map_ref.3, bf16[1,1,2048,384]{3,2,1,0:T(8,128)(2,1)} %fine_hbm.1, bf16[1,1,8,64,6144]{4,3,2,1,0:T(8,128)(2,1)} %prol_hbm.1, bf16[1,1,8,9,64,64]{5,4,3,2,1,0:T(8,128)(2,1)} %op_hbm.1), custom_call_target="tpu_custom_call" | custom-call | tf_op jit(solution)/shard_map/pallas_call | solution.py:308
  10.7 0.0 copy-start
  10.7 20.8 %shard_map.68 = (f32[6152,128]{1,0:T(8,128)S(1)}, f32[128,64]{1,0:T(8,128)S(1)}, f32[1,128]{1,0:T(1,128)S(1)}) custom-call(f32[64,128]{1,0:T(8,128)S(1)} %get-tuple-element.12.rest_ref, bf16[1,1,8,9,64,64]{5,4,3,2,1,0:T(8,128)(2,1)S(1)} %get-tuple-element.13.op_ref, bf16[8,64,6144]{2,1,0:T(8,128)(2,1)S(1)} %get-tuple-element.14.source), custom_call_target="tpu_custom_call" | custom-call | tf_op jit(solution)/shard_map/pallas_call | solution.py:328
  31.5 0.0 copy-done
  31.5 5.2 %shard_map.69 = (bf16[1,1,2048,384]{3,2,1,0:T(8,128)(2,1)}, f32[1,1,8,16,64]{4,3,2,1,0:T(8,128)}, f32[1,16]{1,0:T(1,128)}) custom-call(s32[1,1,2048]{2,1,0:T(1,128)S(1)} %copy-done, f32[6152,128]{1,0:T(8,128)S(1)} %get-tuple-element.15.held, f32[128,64]{1,0:T(8,128)S(1)} %get-tuple-element.16.resid, f32[1,128]{1,0:T(1,128)S(1)} %get-tuple-element.17.norm), custom_call_target="tpu_custom_call" | custom-call | tf_op jit(solution)/shard_map/pallas_call | solution.py:359
Async XLA Ops:
  10.7 20.8 %copy-start = (s32[1,1,2048]{2,1,0:T(1,128)S(1)}, s32[1,1,2048]{2,1,0:T(1,128)}, u32[]{:S(2)}) copy-start(s32[1,1,2048]{2,1,0:T(1,128)} %map_ref.3) | copy-start | bytes 24580
